TPU v7x, 32 devices: a whole 2x2x4 slice. The times are simulated.
32 devices in a mesh: pair: 8 (over y, x, core), slab: 4 (over z).
Axes of the slice: x: 2, y: 2, z: 4, core: 2. Of those that a mesh axis runs over, the one named last changes fastest.
Arguments:
- amplitudes: bfloat16 [8, 8, 160000], P('pair'), may hold values from -6 to 6
- integrals: bfloat16 [160000, 1024], P('pair', 'slab'), may hold values from -0.0390625 to 0.0390625
- virt_irrep: int32 [400], replicated, may hold values from 0 to 7
- occ_energy: float32 [8], replicated, may hold values from -1.2 to -0.3
- slab_energy: float32 [32], replicated, may hold values from 0.1 to 1.5
Outputs:
- update: float32 [8, 8, 32, 32], P('pair', None, 'slab')
All inputs are finite; a program needn't handle non-finite values.
Results may differ from a plain program's by a relative error of at most 0.0003.
Values may be sent and summed in bfloat16 or wider, within the bound.
No kernel may reach another device: no remote copies, remote signals or barrier semaphores. Data moves between devices by JAX's collectives and lax.ppermute only.
A program may use at most 256 MiB of HBM per device.

v0:
```python
import functools
import math

import jax
import jax.numpy as jnp
from jax import lax
from jax.experimental import pallas as pl
from jax.experimental.pallas import tpu as pltpu
from jax.sharding import PartitionSpec as P

IRREPS = 8
MIB = 2**20
SHARE = 0.24
LATE_FLOPS = 10**10


def pack_kernel(rows_local, home, me_ref, start_ref, amps_ref, after_ref, *refs):
    outs, (held, packed, sems) = refs[:-3], refs[-3:]
    _, _, size = packed.shape
    count = sems.shape[0]
    me = me_ref[0]
    start = pl.multiple_of(start_ref[0], 128)
    loads, shifts = [], []
    for dest in range(count):
        first = dest * rows_local // 128 * 128
        shifts.append(dest * rows_local - first)
        width = -(-(shifts[dest] + size) // 128) * 128
        slot = dest ^ me if home else dest
        loads.append(
            pltpu.make_async_copy(
                amps_ref.at[:, pl.ds(start + first, width)], held.at[slot, :, pl.ds(0, width)], sems.at[dest]
            )
        )

    def wanted(dest):
        return (dest ^ me) // 2 == 0 if home else True

    for dest in range(count):
        pl.when(wanted(dest))(loads[dest].start)
    for dest in range(count):

        @pl.when(wanted(dest))
        def _():
            loads[dest].wait()
            packed[dest ^ me] = held[dest ^ me if home else dest, :, shifts[dest] : shifts[dest] + size]

    for k, out in enumerate(outs):
        slot = 0 if home else 2 * k + 2
        out[...] = packed[slot : slot + 2]


def pack(amps, me, start, size, pair_count, home, after=None):
    rows, virt_pairs = amps.shape
    held = (2 if home else pair_count, rows, -(-size // 128) * 128 + 128)
    packed = (held[0], rows, size)
    outs = 1 if home else pair_count // 2 - 1
    vmem = 2 * MIB + 6 * held[0] * rows * held[2]
    return pl.pallas_call(
        functools.partial(pack_kernel, virt_pairs // pair_count, home),
        out_shape=[jax.ShapeDtypeStruct((2, rows, size), amps.dtype)] * outs,
        in_specs=[pl.BlockSpec(memory_space=pltpu.SMEM)] * 2
        + [pl.BlockSpec(memory_space=pltpu.HBM), pl.BlockSpec(memory_space=pl.ANY)],
        out_specs=[pl.BlockSpec(memory_space=pltpu.VMEM)] * outs,
        scratch_shapes=[
            pltpu.VMEM(held, amps.dtype),
            pltpu.VMEM(packed, amps.dtype),
            pltpu.SemaphoreType.DMA((pair_count,)),
        ],
        compiler_params=pltpu.CompilerParams(vmem_limit_bytes=vmem),
        cost_estimate=pl.CostEstimate(flops=0, bytes_accessed=4 * held[0] * rows * size, transcendentals=0),
        name="pack_home" if home else "pack_amplitudes",
    )(me, start, pltpu.with_memory_space_constraint(amps, pltpu.HBM), me if after is None else after)


def mask_kernel(per_step, parts, me_ref, slab_ref, irrep_ref, occ_ref, virt_ref, row_ref, ints_ref, *refs):
    out_ref, select_ref, denominator_ref, table, padded, by_row = refs
    step = pl.program_id(0)
    chunk, cols = ints_ref.shape[1:]
    slab_virt = virt_ref.shape[0]
    first_local = cols // slab_virt
    bits = slab_virt.bit_length() - 1
    me, slab = me_ref[0], slab_ref[0]

    @pl.when(step == 0)
    def _():
        padded[:, : row_ref.shape[1]] = row_ref[...]
        for k in range(padded.shape[1] // 128):
            lanes = slice(k * 128, (k + 1) * 128)
            by_row[lanes] = jnp.transpose(jnp.broadcast_to(padded[:, lanes], (128, 128)))

        col = lax.broadcasted_iota(jnp.int32, (1, cols), 1)
        a_of, b_of = col >> bits, col & (slab_virt - 1)
        irrep_a = irrep_b = jnp.zeros_like(col)
        energy_a = energy_b = jnp.zeros(col.shape, jnp.float32)
        for a in range(first_local):
            irrep_a = jnp.where(a_of == a, irrep_ref[slab * first_local + a], irrep_a)
            energy_a = jnp.where(a_of == a, virt_ref[slab * first_local + a], energy_a)
        for b in range(slab_virt):
            irrep_b = jnp.where(b_of == b, irrep_ref[b], irrep_b)
            energy_b = jnp.where(b_of == b, virt_ref[b], energy_b)
        irrep_ab = irrep_a ^ irrep_b

        for part in range(parts):
            for lanes in (slice(k, k + 128) for k in range(0, cols, 128)):
                needed = by_row[part * chunk : (part + 1) * chunk] ^ irrep_ab[:, lanes]
                for irrep in range(IRREPS):
                    table[irrep * parts + part, :, lanes] = jnp.where(needed == irrep, 1.0, 0.0).astype(table.dtype)

        occupied = denominator_ref.shape[0]
        j_of = lax.broadcasted_iota(jnp.int32, (occupied, cols), 0)
        energy_j = jnp.zeros((occupied, cols), jnp.float32)
        for j in range(occupied):
            energy_j = jnp.where(j_of == j, occ_ref[j], energy_j)
        denominator_ref[...] = energy_a + energy_b - occ_ref[me] - energy_j

        row = lax.broadcasted_iota(jnp.int32, (cols, cols), 0)
        col = lax.broadcasted_iota(jnp.int32, (cols, cols), 1)
        same_a = (row & (slab_virt - 1)) == slab * first_local + (col >> bits)
        for t in range(select_ref.shape[0] // cols):
            same_b = (slab ^ t) * first_local + (row >> bits) == (col & (slab_virt - 1))
            chosen = jnp.where(same_a & same_b, 1.0, 0.0)
            select_ref[t * cols : (t + 1) * cols] = chosen.astype(select_ref.dtype)

    chunks = per_step * pl.num_programs(0)
    for k in range(per_step):
        index = me * chunks + step * per_step + k
        irrep_c = irrep_ref[index // parts]
        out_ref[k] = ints_ref[k] * table[irrep_c * parts + index % parts]


def in_hbm(array):
    return pltpu.with_memory_space_constraint(array, pltpu.HBM)


def mask(integrals, me, slab, virt_irrep, occ_energy, slab_energy):
    virtuals = virt_irrep.shape[0]
    slab_virt = slab_energy.shape[0]
    occupied = occ_energy.shape[0]
    rows_local, cols_local = integrals.shape
    chunk = math.gcd(virtuals, rows_local)
    parts = virtuals // chunk
    chunks = rows_local // chunk
    per_step = next(n for n in (10, 5, 4, 2, 1) if chunks % n == 0)
    padded = -(-virtuals // 128) * 128
    select_rows = slab_virt * slab_virt
    block = pl.BlockSpec((per_step, chunk, cols_local), lambda step: (step, 0, 0))
    scalars = pl.BlockSpec(memory_space=pltpu.SMEM)
    masked, select, denominator = pl.pallas_call(
        functools.partial(mask_kernel, per_step, parts),
        grid=(chunks // per_step,),
        in_specs=[scalars] * 5 + [pl.BlockSpec((1, virtuals), lambda step: (0, 0)), block],
        out_specs=[
            block,
            pl.BlockSpec((select_rows, cols_local), lambda step: (0, 0)),
            pl.BlockSpec((occupied, cols_local), lambda step: (0, 0)),
        ],
        scratch_shapes=[
            pltpu.VMEM((IRREPS * parts, chunk, cols_local), integrals.dtype),
            pltpu.VMEM((1, padded), jnp.int32),
            pltpu.VMEM((padded, 128), jnp.int32),
        ],
        out_shape=[
            pltpu.VMEM((chunks, chunk, cols_local), integrals.dtype),
            jax.ShapeDtypeStruct((select_rows, cols_local), jnp.bfloat16),
            jax.ShapeDtypeStruct((occupied, cols_local), jnp.float32),
        ],
        compiler_params=pltpu.CompilerParams(vmem_limit_bytes=16 * MIB),
        cost_estimate=pl.CostEstimate(
            flops=LATE_FLOPS, bytes_accessed=4 * rows_local * cols_local, transcendentals=0
        ),
        name="mask_integrals",
    )(
        me,
        slab,
        *(in_hbm(array) for array in (virt_irrep, occ_energy, slab_energy, virt_irrep.reshape(1, virtuals))),
        in_hbm(integrals.reshape(chunks, chunk, cols_local)),
    )
    return masked.reshape(rows_local, cols_local), select, denominator


def merge_kernel(*refs):
    parts, home_ref, all_ref, other_ref = refs[:-3], refs[-3], refs[-2], refs[-1]
    size = parts[0].shape[2]
    for k, part in enumerate(parts):
        all_ref[k] = part[...]
        other_ref[:, k * size : (k + 1) * size] = part[1]
    other_ref[:, len(parts) * size :] = home_ref[1]


def merge(parts, home):
    count = len(parts)
    _, rows, size = parts[0].shape
    other = (rows, count * size + home.shape[2])
    vmem = pl.BlockSpec(memory_space=pltpu.VMEM)
    return pl.pallas_call(
        merge_kernel,
        out_shape=[
            jax.ShapeDtypeStruct((count,) + parts[0].shape, home.dtype),
            jax.ShapeDtypeStruct(other, home.dtype),
        ],
        in_specs=[vmem] * (count + 1),
        out_specs=[vmem, vmem],
        compiler_params=pltpu.CompilerParams(vmem_limit_bytes=4 * MIB),
        cost_estimate=pl.CostEstimate(flops=0, bytes_accessed=6 * rows * other[1], transcendentals=0),
        name="merge",
    )(*parts, home)


def other_core_kernel(*refs):
    parts, out_ref = refs[:-2], refs[-1]
    for k, part in enumerate(parts):
        out_ref[k] = part[1]


def for_other_core(parts, after):
    vmem = pl.BlockSpec(memory_space=pltpu.VMEM)
    _, rows, size = parts[0].shape
    out = jax.ShapeDtypeStruct((len(parts), rows, size), parts[0].dtype)
    return pl.pallas_call(
        other_core_kernel,
        out_shape=out,
        in_specs=[vmem] * len(parts) + [pl.BlockSpec(memory_space=pl.ANY)],
        out_specs=vmem,
        compiler_params=pltpu.CompilerParams(vmem_limit_bytes=4 * MIB),
        cost_estimate=pl.CostEstimate(flops=0, bytes_accessed=4 * out.size, transcendentals=0),
        name="for_other_core",
    )(*parts, after)


def contract_kernel(arrays, packed_other, last, start_ref, me_ref, home_ref, home_other_ref, ints_ref, *refs):
    lhs = refs[-2] if last else refs[-1]
    count, rows, size = lhs.shape
    chips = count // 2 - 1
    start = pl.multiple_of(start_ref[0], 128)
    home_first = home_other_ref.shape[1] - home_ref.shape[2]
    columns = pl.ds(start, size)
    lhs[0] = home_ref[0, :, columns]
    lhs[1] = home_other_ref[:, pl.ds(home_first + start, size)]
    mine, refs = refs[:arrays], refs[arrays:]
    for k in range(chips):
        lhs[2 * k + 2] = mine[0][k, 0] if arrays == 1 else mine[k][0]
        if packed_other:
            lhs[2 * k + 3] = home_other_ref[:, k * size : (k + 1) * size]
        else:
            lhs[2 * k + 3] = refs[0][k, 1] if arrays == 1 else refs[0][k]
    refs = refs if packed_other else refs[1:]
    step = 2560
    total = None
    for first in range(0, size, step):
        width = min(step, size - first)
        block = lhs[:, :, first : first + width].reshape(count * rows, width)
        part = jnp.dot(block, ints_ref[pl.ds(start + first, width)], preferred_element_type=jnp.float32)
        total = part if total is None else total + part
    if not last:
        before, out_ref = refs[:-2], refs[-2]
        out_ref[...] = total + before[0][...] if before else total
        return
    before_ref, out_ref, _, partial = refs
    me = me_ref[0]
    partial[...] = (total + before_ref[...]).reshape(partial.shape)
    for p in range(count):
        out_ref[p, :count] = partial[p ^ me]
        for i in range(count):
            out_ref[p, count + i : count + i + 1] = partial[i ^ me, p : p + 1]


def contract(mine, others, home, home_other, ints, start, me, before=None, last=False, flops=0):
    occupied, size = mine[0].shape[-2:]
    cols = ints.shape[1]
    vmem = pl.BlockSpec(memory_space=pltpu.VMEM)
    operands = [*mine, *others] + ([] if before is None else [before])
    scratch = [pltpu.VMEM((occupied, occupied, size), home.dtype)]
    if last:
        out_shape = jax.ShapeDtypeStruct((occupied, 2 * occupied, cols), jnp.float32)
        scratch.append(pltpu.VMEM((occupied, occupied, cols), jnp.float32))
    else:
        out_shape = jax.ShapeDtypeStruct((occupied * occupied, cols), jnp.float32)
    return pl.pallas_call(
        functools.partial(contract_kernel, len(mine), not others, last),
        out_shape=out_shape,
        in_specs=[pl.BlockSpec(memory_space=pltpu.SMEM)] * 2 + [vmem] * (3 + len(operands)),
        out_specs=vmem,
        scratch_shapes=scratch,
        compiler_params=pltpu.CompilerParams(vmem_limit_bytes=4 * MIB + 16 * occupied * occupied * cols + 4 * occupied * occupied * size),
        cost_estimate=pl.CostEstimate(
            flops=2 * occupied * occupied * size * cols + flops,
            bytes_accessed=2 * size * (cols + occupied * occupied),
            transcendentals=0,
        ),
        name="contract",
    )(start, me, home, home_other, pltpu.with_memory_space_constraint(ints, pltpu.VMEM), *operands)


def select_exactly(values, select):
    rows = values.shape[0]
    high = values.astype(jnp.bfloat16)
    rest = values - high.astype(jnp.float32)
    middle = rest.astype(jnp.bfloat16)
    low = (rest - middle.astype(jnp.float32)).astype(jnp.bfloat16)
    terms = [jnp.dot(term, select, preferred_element_type=jnp.float32) for term in (high, middle, low)]
    return terms[0] + terms[1] + terms[2]


def add_kernel(parts_ref, ladder_ref, mirror_ref):
    total = parts_ref[0]
    for q in range(1, parts_ref.shape[0]):
        total = total + parts_ref[q]
    half = total.shape[0] // 2
    ladder_ref[...] = total[:half]
    mirror_ref[...] = total[half:]


def add_parts(parts):
    _, rows, cols = parts.shape
    half = jax.ShapeDtypeStruct((rows // 2, cols), jnp.float32)
    vmem = pl.BlockSpec(memory_space=pltpu.VMEM)
    return pl.pallas_call(
        add_kernel,
        out_shape=[half, half],
        in_specs=[vmem],
        out_specs=[vmem, vmem],
        compiler_params=pltpu.CompilerParams(vmem_limit_bytes=4 * MIB),
        cost_estimate=pl.CostEstimate(flops=parts.size, bytes_accessed=4 * parts.size, transcendentals=0),
        name="add_parts",
    )(parts)


def finish_kernel(ladder_ref, denominator_ref, select_ref, *refs):
    mirrors, out_ref = refs[:-1], refs[-1]
    mirror = select_exactly(jnp.concatenate([ref[...] for ref in mirrors], axis=1), select_ref[...])
    update = (ladder_ref[...] + mirror) / denominator_ref[...]
    _, first_local, slab_virt = out_ref.shape
    for a in range(first_local):
        out_ref[:, a, :] = update[:, a * slab_virt : (a + 1) * slab_virt]


def finish(ladder, mirrors, denominator, select, first_local, slab_virt):
    rows = ladder.shape[0]
    return pl.pallas_call(
        finish_kernel,
        out_shape=jax.ShapeDtypeStruct((rows, first_local, slab_virt), jnp.float32),
        in_specs=[pl.BlockSpec(memory_space=pltpu.VMEM)] * (3 + len(mirrors)),
        out_specs=pl.BlockSpec(memory_space=pltpu.VMEM),
        compiler_params=pltpu.CompilerParams(vmem_limit_bytes=6 * MIB),
        cost_estimate=pl.CostEstimate(flops=6 * rows * select.size, bytes_accessed=2 * select.size, transcendentals=0),
        name="finish",
    )(ladder, denominator, select, *mirrors)


def swap(values, axis, bits):
    return lax.ppermute(values, axis, [(p, p ^ bits) for p in range(lax.axis_size(axis))])


def local(amplitudes, integrals, virt_irrep, occ_energy, slab_energy):
    pair_count = lax.axis_size("pair")
    slab_count = lax.axis_size("slab")
    occ_local, occupied, virt_pairs = amplitudes.shape
    rows_local, cols_local = integrals.shape
    slab_virt = slab_energy.shape[0]
    first_local = slab_virt // slab_count
    assert occ_local == 1
    slab_index = lax.axis_index("slab").astype(jnp.int32)
    me = lax.axis_index("pair").astype(jnp.int32).reshape(1)
    slab = slab_index.reshape(1)

    shared = int(SHARE * rows_local) // 128 * 128
    parity = slab_index % 2
    own = (parity * shared).reshape(1)
    other = ((1 - parity) * shared).reshape(1)
    rest = jnp.full((1,), 2 * shared, jnp.int32)
    whole = jnp.zeros((1,), jnp.int32)
    amps = amplitudes.reshape(occupied, virt_pairs)
    chips = [2 * k for k in range(1, pair_count // 2)]

    parts = pack(amps, me, own, shared, pair_count, False)
    own_mine = [swap(part, "pair", bits) for part, bits in zip(parts, chips)]
    parts = pack(amps, me, rest, rows_local - 2 * shared, pair_count, False, parts[-1])
    rest_mine = [swap(part, "pair", bits) for part, bits in zip(parts, chips)]
    (home,) = pack(amps, me, whole, rows_local, pair_count, True, parts[-1])

    own_mine, for_other = merge(own_mine, home)
    other_mine = swap(own_mine, "slab", 1)
    home_other = swap(for_other, "pair", 1)
    other_others = swap(other_mine, "pair", 1)
    masked, select, denominator = mask(integrals, me, slab, virt_irrep, occ_energy, slab_energy)
    rest_others = swap(for_other_core(rest_mine, denominator), "pair", 1)
    partial = contract([own_mine], [], home, home_other, masked, own, me)
    partial = contract(rest_mine, [rest_others], home, home_other, masked, rest, me, partial)
    parts = contract([other_mine], [other_others], home, home_other, masked, other, me, partial, True)

    parts = lax.all_to_all(parts, "pair", split_axis=0, concat_axis=0, tiled=True)
    ladder, mirror = add_parts(parts)
    mirrors = [mirror] + [swap(mirror, "slab", bits) for bits in range(1, slab_count)]
    update = finish(ladder, mirrors, denominator, select, first_local, slab_virt)
    return update.reshape(occ_local, occupied, first_local, slab_virt)


def solution(mesh):
    placed = (P("pair", None, None), P("pair", "slab"), P(), P(), P())
    return jax.shard_map(
        local, mesh=mesh, in_specs=placed, out_specs=P("pair", None, "slab", None), check_vma=False
    )
```

profile of v0, /device:TPU:0, one launch (start us, length us, event | category | flops | bytes accessed | tf_op | source)
XLA Modules:
  0.0 60.8 jit_solution(6296958771369832133)
XLA Ops:
  0.0 1.6 %pack_amplitudes.2 = (bf16[2,8,4736]{2,1,0:T(8,128)(2,1)S(1)}, bf16[2,8,4736]{2,1,0:T(8,128)(2,1)S(1)}, bf16[2,8,4736]{2,1,0:T(8,128)(2,1)S(1)}) custom-call(s32[1]{0:T(128)} %bitcast.1.me_ref.after_ref, s32[1]{0:T(128)} %bitcast.3.start_ref, bf16[8,160000]{1,0:T(8,128)(2,1)} %bitcast.12, s32[1]{0:T(128)} %bitcast.1.me_ref.after_ref), custom_call_target="tpu_custom_call" | custom-call | bytes 1212416 | tf_op jit(solution)/shard_map/pack_amplitudes/pallas_call | solution.py:58
  1.6 3.0 %collective-permute-start = (bf16[2,8,4736]{2,1,0:T(8,128)(2,1)S(1)}, bf16[2,8,4736]{2,1,0:T(8,128)(2,1)S(1)}, u32[]{:S(2)}, u32[]{:S(2)}) collective-permute-start(bf16[2,8,4736]{2,1,0:T(8,128)(2,1)S(1)} %get-tuple-element.20), channel_id=1, source_target_pairs={{0,8},{4,12},{8,0},{12,4},{16,24},{20,28},{24,16},{28,20},{1,9},{5... | collective-permute-start | bytes 454664 | tf_op jit(solution)/shard_map/ppermute | solution.py:351
  4.6 1.5 %collective-permute-start.1 = (bf16[2,8,4736]{2,1,0:T(8,128)(2,1)S(1)}, bf16[2,8,4736]{2,1,0:T(8,128)(2,1)S(1)}, u32[]{:S(2)}, u32[]{:S(2)}) collective-permute-start(bf16[2,8,4736]{2,1,0:T(8,128)(2,1)S(1)} %get-tuple-element.21), channel_id=1, source_target_pairs={{0,16},{4,20},{8,24},{12,28},{16,0},{20,4},{24,8},{28,12},{1,17},{... | collective-permute-start | bytes 454664 | tf_op jit(solution)/shard_map/ppermute | solution.py:351
  6.1 1.8 %pack_amplitudes.3 = (bf16[2,8,10528]{2,1,0:T(8,128)(2,1)S(1)}, bf16[2,8,10528]{2,1,0:T(8,128)(2,1)S(1)}, bf16[2,8,10528]{2,1,0:T(8,128)(2,1)S(1)}) custom-call(s32[1]{0:T(128)} %bitcast.1.me_ref.after_ref, s32[1]{0:T(128)} %constant.28.clone.1.start_ref, bf16[8,160000]{1,0:T(8,128)(2,1)} %bitcast.13, bf16[2,8,4736]{2,1,0:T(8,128)(2,1)S(1)} %get-tuple-element.18.after_ref), custom_call_target="tpu_custom_call" | custom-call | bytes 2695168 | tf_op jit(solution)/shard_map/pack_amplitudes/pallas_call | solution.py:58
  8.0 2.0 %collective-permute-start.6 = (bf16[2,8,10528]{2,1,0:T(8,128)(2,1)S(1)}, bf16[2,8,10528]{2,1,0:T(8,128)(2,1)S(1)}, u32[]{:S(2)}, u32[]{:S(2)}) collective-permute-start(bf16[2,8,10528]{2,1,0:T(8,128)(2,1)S(1)} %get-tuple-element.25), channel_id=1, source_target_pairs={{0,8},{4,12},{8,0},{12,4},{16,24},{20,28},{24,16},{28,20},{1,9},{5... | collective-permute-start | bytes 1010696 | tf_op jit(solution)/shard_map/ppermute | solution.py:351
  10.0 1.5 %collective-permute-start.8 = (bf16[2,8,10528]{2,1,0:T(8,128)(2,1)S(1)}, bf16[2,8,10528]{2,1,0:T(8,128)(2,1)S(1)}, u32[]{:S(2)}, u32[]{:S(2)}) collective-permute-start(bf16[2,8,10528]{2,1,0:T(8,128)(2,1)S(1)} %get-tuple-element.19.after_ref), channel_id=1, source_target_pairs={{0,24},{4,28},{8,16},{12,20},{16,8},{20,12},{24,0},{28,4},{1,25},{... | collective-permute-start | bytes 1010696 | tf_op jit(solution)/shard_map/ppermute | solution.py:351
  11.5 1.3 %pack_home.1.refs_3_.home_ref = bf16[2,8,20000]{2,1,0:T(8,128)(2,1)S(1)} custom-call(s32[1]{0:T(128)} %bitcast.1.me_ref.after_ref, s32[1]{0:T(128)} %constant.27.clone.1.start_ref, bf16[8,160000]{1,0:T(8,128)(2,1)} %bitcast.14, bf16[2,8,10528]{2,1,0:T(8,128)(2,1)S(1)} %get-tuple-element.19.after_ref), custom_call_target="tpu_custom_call" | custom-call | bytes 1280000 | tf_op jit(solution)/shard_map/pack_home/pallas_call | solution.py:58
  12.9 1.0 %collective-permute-done.2.refs_2_ = bf16[2,8,4736]{2,1,0:T(8,128)(2,1)S(1)} collective-permute-done((bf16[2,8,4736]{2,1,0:T(8,128)(2,1)S(1)}, bf16[2,8,4736]{2,1,0:T(8,128)(2,1)S(1)}, u32[]{:S(2)}, u32[]{:S(2)}) %collective-permute-start.2) | collective-permute-done | bytes 151584 | tf_op jit(solution)/shard_map/ppermute | solution.py:351
  13.9 0.9 %merge.1 = (bf16[3,2,8,4736]{3,2,1,0:T(8,128)(2,1)S(1)}, bf16[8,34208]{1,0:T(8,128)(2,1)}) custom-call(bf16[2,8,4736]{2,1,0:T(8,128)(2,1)S(1)} %collective-permute-done.refs_0_, bf16[2,8,4736]{2,1,0:T(8,128)(2,1)S(1)} %collective-permute-done.1.refs_1_, bf16[2,8,4736]{2,1,0:T(8,128)(2,1)S(1)} %collective-permute-done.2.refs_2_, ...), custom_call_target="tpu_custom_call" | custom-call | bytes 1641984 | tf_op jit(solution)/shard_map/merge/pallas_call | solution.py:195
  14.8 1.6 %collective-permute-start.4 = (bf16[3,2,8,4736]{3,2,1,0:T(8,128)(2,1)S(1)}, bf16[3,2,8,4736]{3,2,1,0:T(8,128)(2,1)}, u32[]{:S(2)}, u32[]{:S(2)}) collective-permute-start(bf16[3,2,8,4736]{3,2,1,0:T(8,128)(2,1)S(1)} %get-tuple-element.24.refs_0_), channel_id=1, source_target_pairs={{0,1},{1,0},{2,3},{3,2},{4,5},{5,4},{6,7},{7,6},{8,9},{9,8},{10,11... | collective-permute-start | bytes 1363976 | tf_op jit(solution)/shard_map/ppermute | solution.py:351
  16.4 6.3 %mask_integrals.1 = (bf16[50,400,256]{2,1,0:T(8,128)(2,1)S(1)}, bf16[1024,256]{1,0:T(8,128)(2,1)S(1)}, f32[8,256]{1,0:T(8,128)S(1)}) custom-call(s32[1]{0:T(128)} %bitcast.1.me_ref.after_ref, s32[1]{0:T(128)} %bitcast.4.slab_ref, s32[400]{0:T(512)} %irrep_ref.1, f32[8]{0:T(128)} %occ_ref.1, f32[32]{0:T(128)} %virt_ref.1, s32[1,400]{1,0:T(1,128)} %bitcast.16, ...), custom_call_target="tpu_custom_call" | custom-call | flops 10000000000 | bytes 20480000 | tf_op jit(solution)/shard_map/mask_integrals/pallas_call | solution.py:148
  22.8 3.9 %copy-done = bf16[50,400,256]{2,1,0:T(8,128)(2,1)} copy-done((bf16[50,400,256]{2,1,0:T(8,128)(2,1)}, bf16[50,400,256]{2,1,0:T(8,128)(2,1)S(1)}, u32[]{:S(2)}) %copy-start) | copy-done | bytes 10240024
  26.6 1.9 %collective-permute-done.7.refs_1_ = bf16[2,8,10528]{2,1,0:T(8,128)(2,1)S(1)} collective-permute-done((bf16[2,8,10528]{2,1,0:T(8,128)(2,1)S(1)}, bf16[2,8,10528]{2,1,0:T(8,128)(2,1)S(1)}, u32[]{:S(2)}, u32[]{:S(2)}) %collective-permute-start.7) | collective-permute-done | bytes 336928 | tf_op jit(solution)/shard_map/ppermute | solution.py:351
  29.1 3.9 %copy-done.1 = bf16[50,400,256]{2,1,0:T(8,128)(2,1)S(1)} copy-done((bf16[50,400,256]{2,1,0:T(8,128)(2,1)S(1)}, bf16[50,400,256]{2,1,0:T(8,128)(2,1)}, u32[]{:S(2)}) %copy-start.1) | copy-done | bytes 10240024
  33.0 1.0 %copy-done.4 = bf16[3,2,8,4736]{3,2,1,0:T(8,128)(2,1)S(1)} copy-done((bf16[3,2,8,4736]{3,2,1,0:T(8,128)(2,1)S(1)}, bf16[3,2,8,4736]{3,2,1,0:T(8,128)(2,1)}, u32[]{:S(2)}) %copy-start.4) | copy-done | bytes 454680
  34.5 3.4 %copy-done.2 = bf16[50,400,256]{2,1,0:T(8,128)(2,1)S(1)} copy-done((bf16[50,400,256]{2,1,0:T(8,128)(2,1)S(1)}, bf16[50,400,256]{2,1,0:T(8,128)(2,1)}, u32[]{:S(2)}) %copy-start.2) | copy-done | bytes 10240024
  38.0 2.1 %contract.4.refs_2_ = f32[64,256]{1,0:T(8,128)S(1)} custom-call(s32[1]{0:T(128)} %constant.28.clone.1.start_ref, s32[1]{0:T(128)} %bitcast.1.me_ref.after_ref, bf16[2,8,20000]{2,1,0:T(8,128)(2,1)S(1)} %pack_home.1.refs_3_.home_ref, bf16[8,34208]{1,0:T(8,128)(2,1)S(1)} %collective-permute-done.3.home_other_ref, bf16[20000,256]{1,0:T(8,128)(2,1)S(1)} %bitcast.10, ...), custom_call_target="tpu_custom_call" | custom-call | flops 344981504 | bytes 6737920 | tf_op jit(solution)/shard_map/contract/pallas_call | solution.py:278
  40.1 1.7 %contract.5 = f32[8,16,256]{2,1,0:T(8,128)S(1)} custom-call(s32[1]{0:T(128)} %bitcast.start_ref, s32[1]{0:T(128)} %bitcast.1.me_ref.after_ref, bf16[2,8,20000]{2,1,0:T(8,128)(2,1)S(1)} %pack_home.1.refs_3_.home_ref, bf16[8,34208]{1,0:T(8,128)(2,1)S(1)} %collective-permute-done.3.home_other_ref, bf16[20000,256]{1,0:T(8,128)(2,1)S(1)} %bitcast.11, ...), custom_call_target="tpu_custom_call" | custom-call | flops 155189248 | bytes 3031040 | tf_op jit(solution)/shard_map/contract/pallas_call | solution.py:278
  41.8 8.2 %all_to_all.5.parts_ref = f32[8,16,256]{2,1,0:T(8,128)S(1)} all-to-all(f32[8,16,256]{2,1,0:T(8,128)S(1)} %contract.5), channel_id=1, replica_groups=mesh['pair'=8,'slab'=4] {'pair'}, dimensions={0} | all-to-all | bytes 262144 | tf_op jit(solution)/shard_map/all_to_all | solution.py:391
  50.0 1.6 %collective-permute-start.10 = (f32[8,256]{1,0:T(8,128)S(1)}, f32[8,256]{1,0:T(8,128)S(1)}, u32[]{:S(2)}, u32[]{:S(2)}) collective-permute-start(f32[8,256]{1,0:T(8,128)S(1)} %get-tuple-element.30.refs_0_), channel_id=1, source_target_pairs={{0,1},{1,0},{2,3},{3,2},{4,5},{5,4},{6,7},{7,6},{8,9},{9,8},{10,11... | collective-permute-start | bytes 24584 | tf_op jit(solution)/shard_map/ppermute | solution.py:351
  51.7 2.6 %collective-permute-start.11 = (f32[8,256]{1,0:T(8,128)S(1)}, f32[8,256]{1,0:T(8,128)S(1)}, u32[]{:S(2)}, u32[]{:S(2)}) collective-permute-start(f32[8,256]{1,0:T(8,128)S(1)} %get-tuple-element.30.refs_0_), channel_id=1, source_target_pairs={{0,2},{1,3},{2,0},{3,1},{4,6},{5,7},{6,4},{7,5},{8,10},{9,11},{10,... | collective-permute-start | bytes 24584 | tf_op jit(solution)/shard_map/ppermute | solution.py:351
  54.5 1.7 %collective-permute-done.11.refs_2_ = f32[8,256]{1,0:T(8,128)S(1)} collective-permute-done((f32[8,256]{1,0:T(8,128)S(1)}, f32[8,256]{1,0:T(8,128)S(1)}, u32[]{:S(2)}, u32[]{:S(2)}) %collective-permute-start.11) | collective-permute-done | bytes 8224 | tf_op jit(solution)/shard_map/ppermute | solution.py:351
  56.2 3.5 %collective-permute-done.12.refs_3_ = f32[8,256]{1,0:T(8,128)S(1)} collective-permute-done((f32[8,256]{1,0:T(8,128)S(1)}, f32[8,256]{1,0:T(8,128)S(1)}, u32[]{:S(2)}, u32[]{:S(2)}) %collective-permute-start.12) | collective-permute-done | bytes 8224 | tf_op jit(solution)/shard_map/ppermute | solution.py:351
  59.7 1.1 %finish.1 = f32[8,8,32]{2,1,0:T(8,128)} custom-call(f32[8,256]{1,0:T(8,128)S(1)} %get-tuple-element.28.ladder_ref, f32[8,256]{1,0:T(8,128)S(1)} %get-tuple-element.27.refs_3_.denominator_ref, bf16[1024,256]{1,0:T(8,128)(2,1)S(1)} %get-tuple-element.29.select_ref, f32[8,256]{1,0:T(8,128)S(1)} %get-tuple-element.30.refs_0_, ...), custom_call_target="tpu_custom_call" | custom-call | flops 12582912 | bytes 524288 | tf_op jit(solution)/shard_map/finish/pallas_call | solution.py:339
  (24 shorter events, 1.5 us)
Async XLA Ops:
  1.6 11.2 %collective-permute-start = (bf16[2,8,4736]{2,1,0:T(8,128)(2,1)S(1)}, bf16[2,8,4736]{2,1,0:T(8,128)(2,1)S(1)}, u32[]{:S(2)}, u32[]{:S(2)}) collective-permute-start(bf16[2,8,4736]{2,1,0:T(8,128)(2,1)S(1)} %get-tuple-element.20), channel_id=1, source_target_pairs={{0,8},{4,12},{8,0},{12,4},{16,24},{20,28},{24,16},{28,20},{1,9},{5... | collective-permute-start | bytes 454664 | tf_op jit(solution)/shard_map/ppermute | solution.py:351
  4.6 8.4 %collective-permute-start.1 = (bf16[2,8,4736]{2,1,0:T(8,128)(2,1)S(1)}, bf16[2,8,4736]{2,1,0:T(8,128)(2,1)S(1)}, u32[]{:S(2)}, u32[]{:S(2)}) collective-permute-start(bf16[2,8,4736]{2,1,0:T(8,128)(2,1)S(1)} %get-tuple-element.21), channel_id=1, source_target_pairs={{0,16},{4,20},{8,24},{12,28},{16,0},{20,4},{24,8},{28,12},{1,17},{... | collective-permute-start | bytes 454664 | tf_op jit(solution)/shard_map/ppermute | solution.py:351
  6.1 7.8 %collective-permute-start.2 = (bf16[2,8,4736]{2,1,0:T(8,128)(2,1)S(1)}, bf16[2,8,4736]{2,1,0:T(8,128)(2,1)S(1)}, u32[]{:S(2)}, u32[]{:S(2)}) collective-permute-start(bf16[2,8,4736]{2,1,0:T(8,128)(2,1)S(1)} %get-tuple-element.18.after_ref), channel_id=1, source_target_pairs={{0,24},{4,28},{8,16},{12,20},{16,8},{20,12},{24,0},{28,4},{1,25},{... | collective-permute-start | bytes 454664 | tf_op jit(solution)/shard_map/ppermute | solution.py:351
  8.0 18.7 %collective-permute-start.6 = (bf16[2,8,10528]{2,1,0:T(8,128)(2,1)S(1)}, bf16[2,8,10528]{2,1,0:T(8,128)(2,1)S(1)}, u32[]{:S(2)}, u32[]{:S(2)}) collective-permute-start(bf16[2,8,10528]{2,1,0:T(8,128)(2,1)S(1)} %get-tuple-element.25), channel_id=1, source_target_pairs={{0,8},{4,12},{8,0},{12,4},{16,24},{20,28},{24,16},{28,20},{1,9},{5... | collective-permute-start | bytes 1010696 | tf_op jit(solution)/shard_map/ppermute | solution.py:351
  10.0 18.5 %collective-permute-start.8 = (bf16[2,8,10528]{2,1,0:T(8,128)(2,1)S(1)}, bf16[2,8,10528]{2,1,0:T(8,128)(2,1)S(1)}, u32[]{:S(2)}, u32[]{:S(2)}) collective-permute-start(bf16[2,8,10528]{2,1,0:T(8,128)(2,1)S(1)} %get-tuple-element.19.after_ref), channel_id=1, source_target_pairs={{0,24},{4,28},{8,16},{12,20},{16,8},{20,12},{24,0},{28,4},{1,25},{... | collective-permute-start | bytes 1010696 | tf_op jit(solution)/shard_map/ppermute | solution.py:351
  12.8 15.7 %collective-permute-start.7 = (bf16[2,8,10528]{2,1,0:T(8,128)(2,1)S(1)}, bf16[2,8,10528]{2,1,0:T(8,128)(2,1)S(1)}, u32[]{:S(2)}, u32[]{:S(2)}) collective-permute-start(bf16[2,8,10528]{2,1,0:T(8,128)(2,1)S(1)} %get-tuple-element.26), channel_id=1, source_target_pairs={{0,16},{4,20},{8,24},{12,28},{16,0},{20,4},{24,8},{28,12},{1,17},{... | collective-permute-start | bytes 1010696 | tf_op jit(solution)/shard_map/ppermute | solution.py:351
  14.8 7.9 %copy-start.3 = (bf16[3,2,8,4736]{3,2,1,0:T(8,128)(2,1)}, bf16[3,2,8,4736]{3,2,1,0:T(8,128)(2,1)S(1)}, u32[]{:S(2)}) copy-start(bf16[3,2,8,4736]{3,2,1,0:T(8,128)(2,1)S(1)} %get-tuple-element.24.refs_0_) | copy-start | bytes 1363972
  14.8 14.3 %collective-permute-start.3 = (bf16[8,34208]{1,0:T(8,128)(2,1)}, bf16[8,34208]{1,0:T(8,128)(2,1)S(1)}, u32[]{:S(2)}, u32[]{:S(2)}) collective-permute-start(bf16[8,34208]{1,0:T(8,128)(2,1)} %get-tuple-element.22), channel_id=1, source_target_pairs={{0,4},{4,0},{8,12},{12,8},{16,20},{20,16},{24,28},{28,24},{1,5},{5... | collective-permute-start | bytes 1641992 | tf_op jit(solution)/shard_map/ppermute | solution.py:351
  14.8 13.8 %collective-permute-start.4 = (bf16[3,2,8,4736]{3,2,1,0:T(8,128)(2,1)S(1)}, bf16[3,2,8,4736]{3,2,1,0:T(8,128)(2,1)}, u32[]{:S(2)}, u32[]{:S(2)}) collective-permute-start(bf16[3,2,8,4736]{3,2,1,0:T(8,128)(2,1)S(1)} %get-tuple-element.24.refs_0_), channel_id=1, source_target_pairs={{0,1},{1,0},{2,3},{3,2},{4,5},{5,4},{6,7},{7,6},{8,9},{9,8},{10,11... | collective-permute-start | bytes 1363976 | tf_op jit(solution)/shard_map/ppermute | solution.py:351
  22.8 3.9 %copy-start = (bf16[50,400,256]{2,1,0:T(8,128)(2,1)}, bf16[50,400,256]{2,1,0:T(8,128)(2,1)S(1)}, u32[]{:S(2)}) copy-start(bf16[50,400,256]{2,1,0:T(8,128)(2,1)S(1)} %get-tuple-element.23) | copy-start | bytes 30720004
  28.5 6.0 %collective-permute-start.9 = (bf16[3,8,10528]{2,1,0:T(8,128)(2,1)S(1)}, bf16[3,8,10528]{2,1,0:T(8,128)(2,1)}, u32[]{:S(2)}, u32[]{:S(2)}) collective-permute-start(bf16[3,8,10528]{2,1,0:T(8,128)(2,1)S(1)} %for_other_core.1), channel_id=1, source_target_pairs={{0,4},{4,0},{8,12},{12,8},{16,20},{20,16},{24,28},{28,24},{1,5},{5... | collective-permute-start | bytes 1516040 | tf_op jit(solution)/shard_map/ppermute | solution.py:351
  28.6 11.5 %collective-permute-start.5 = (bf16[3,2,8,4736]{3,2,1,0:T(8,128)(2,1)}, bf16[3,2,8,4736]{3,2,1,0:T(8,128)(2,1)}, u32[]{:S(2)}, u32[]{:S(2)}) collective-permute-start(bf16[3,2,8,4736]{3,2,1,0:T(8,128)(2,1)} %collective-permute-done.4.refs_0_), channel_id=1, source_target_pairs={{0,4},{4,0},{8,12},{12,8},{16,20},{20,16},{24,28},{28,24},{1,5},{5... | collective-permute-start | bytes 1363976 | tf_op jit(solution)/shard_map/ppermute | solution.py:351
  29.1 3.9 %copy-start.1 = (bf16[50,400,256]{2,1,0:T(8,128)(2,1)S(1)}, bf16[50,400,256]{2,1,0:T(8,128)(2,1)}, u32[]{:S(2)}) copy-start(bf16[50,400,256]{2,1,0:T(8,128)(2,1)} %copy-done) | copy-start | bytes 30720004
  33.0 1.0 %copy-start.4 = (bf16[3,2,8,4736]{3,2,1,0:T(8,128)(2,1)S(1)}, bf16[3,2,8,4736]{3,2,1,0:T(8,128)(2,1)}, u32[]{:S(2)}) copy-start(bf16[3,2,8,4736]{3,2,1,0:T(8,128)(2,1)} %copy-done.3) | copy-start | bytes 1363972
  34.1 3.9 %copy-start.2 = (bf16[50,400,256]{2,1,0:T(8,128)(2,1)S(1)}, bf16[50,400,256]{2,1,0:T(8,128)(2,1)}, u32[]{:S(2)}) copy-start(bf16[50,400,256]{2,1,0:T(8,128)(2,1)} %copy-done) | copy-start | bytes 30720004
  50.0 4.5 %collective-permute-start.10 = (f32[8,256]{1,0:T(8,128)S(1)}, f32[8,256]{1,0:T(8,128)S(1)}, u32[]{:S(2)}, u32[]{:S(2)}) collective-permute-start(f32[8,256]{1,0:T(8,128)S(1)} %get-tuple-element.30.refs_0_), channel_id=1, source_target_pairs={{0,1},{1,0},{2,3},{3,2},{4,5},{5,4},{6,7},{7,6},{8,9},{9,8},{10,11... | collective-permute-start | bytes 24584 | tf_op jit(solution)/shard_map/ppermute | solution.py:351
  51.7 4.5 %collective-permute-start.11 = (f32[8,256]{1,0:T(8,128)S(1)}, f32[8,256]{1,0:T(8,128)S(1)}, u32[]{:S(2)}, u32[]{:S(2)}) collective-permute-start(f32[8,256]{1,0:T(8,128)S(1)} %get-tuple-element.30.refs_0_), channel_id=1, source_target_pairs={{0,2},{1,3},{2,0},{3,1},{4,6},{5,7},{6,4},{7,5},{8,10},{9,11},{10,... | collective-permute-start | bytes 24584 | tf_op jit(solution)/shard_map/ppermute | solution.py:351
  54.2 5.4 %collective-permute-start.12 = (f32[8,256]{1,0:T(8,128)S(1)}, f32[8,256]{1,0:T(8,128)S(1)}, u32[]{:S(2)}, u32[]{:S(2)}) collective-permute-start(f32[8,256]{1,0:T(8,128)S(1)} %get-tuple-element.30.refs_0_), channel_id=1, source_target_pairs={{0,3},{1,2},{2,1},{3,0},{4,7},{5,6},{6,5},{7,4},{8,11},{9,10},{10,... | collective-permute-start | bytes 24584 | tf_op jit(solution)/shard_map/ppermute | solution.py:351
where the time goes:
time: 61.2 us; the launch traced here: 60.8 us
  Pallas kernels  17.3 us (28%)
  starting transfers between devices  14.7 us (24%)
  local copies, waits for them, and re-layouts  12.2 us (20%)
  blocking collectives  8.22 us (13%)
  waiting for transfers between devices  8.08 us (13%)
    ppermute x13, starting transfers between devices, swap(): lax.ppermute(values, axis, [(p, p ^ bits) for p in range(lax.axis_size(ax...  14.7 us
    unnamed x10, local copies, waits for them, and re-layouts  12.2 us
    all_to_all x1, blocking collectives, local(): lax.all_to_all(parts, 'pair', split_axis=0, concat_axis=0, tiled=True)  8.22 us
    ppermute x13, waiting for transfers between devices, swap(): lax.ppermute(values, axis, [(p, p ^ bits) for p in range(lax.axis_size(ax...  8.08 us
    pallas_call x1, Pallas kernels, mask(): pl.pallas_call(functools.partial(mask_kernel, per_step, parts), grid=(chu...  6.33 us
    pallas_call x3, Pallas kernels, pack(): pl.pallas_call(functools.partial(pack_kernel, virt_pairs // pair_count, h...  4.75 us
    pallas_call x3, Pallas kernels, contract(): pl.pallas_call(functools.partial(contract_kernel, len(mine), not others,...  4.25 us
  transfers between devices with their start and end apart: 13, of which 4 were waited for; matrix products, arithmetic and copies ran while one was open for 0% of the time, Pallas kernels for 21%

commit v1 on v0

--- a/solution.py
+++ b/solution.py
@@ -14,12 +14,18 @@
 LATE_FLOPS = 10**10
 
 
-def pack_kernel(rows_local, home, me_ref, start_ref, amps_ref, after_ref, *refs):
+def start_of(part, slab_ref, shared):
+    parity = slab_ref[0] % 2
+    return pl.multiple_of({"own": parity * shared, "other": (1 - parity) * shared, "rest": 2 * shared, "all": 0}[part], 128)
+
+
+def pack_kernel(rows_local, shared, which, me_ref, slab_ref, amps_ref, after_ref, *refs):
     outs, (held, packed, sems) = refs[:-3], refs[-3:]
     _, _, size = packed.shape
     count = sems.shape[0]
+    home = which == "all"
     me = me_ref[0]
-    start = pl.multiple_of(start_ref[0], 128)
+    start = start_of(which, slab_ref, shared)
     loads, shifts = [], []
     for dest in range(count):
         first = dest * rows_local // 128 * 128
@@ -49,14 +55,17 @@
         out[...] = packed[slot : slot + 2]
 
 
-def pack(amps, me, start, size, pair_count, home, after=None):
+def pack(amps, me, slab, shared, which, pair_count, after=None):
     rows, virt_pairs = amps.shape
+    rows_local = virt_pairs // pair_count
+    home = which == "all"
+    size = {"own": shared, "rest": rows_local - 2 * shared, "all": rows_local}[which]
     held = (2 if home else pair_count, rows, -(-size // 128) * 128 + 128)
     packed = (held[0], rows, size)
     outs = 1 if home else pair_count // 2 - 1
     vmem = 2 * MIB + 6 * held[0] * rows * held[2]
     return pl.pallas_call(
-        functools.partial(pack_kernel, virt_pairs // pair_count, home),
+        functools.partial(pack_kernel, rows_local, shared, which),
         out_shape=[jax.ShapeDtypeStruct((2, rows, size), amps.dtype)] * outs,
         in_specs=[pl.BlockSpec(memory_space=pltpu.SMEM)] * 2
         + [pl.BlockSpec(memory_space=pltpu.HBM), pl.BlockSpec(memory_space=pl.ANY)],
@@ -69,7 +78,7 @@
         compiler_params=pltpu.CompilerParams(vmem_limit_bytes=vmem),
         cost_estimate=pl.CostEstimate(flops=0, bytes_accessed=4 * held[0] * rows * size, transcendentals=0),
         name="pack_home" if home else "pack_amplitudes",
-    )(me, start, pltpu.with_memory_space_constraint(amps, pltpu.HBM), me if after is None else after)
+    )(me, slab, pltpu.with_memory_space_constraint(amps, pltpu.HBM), me if after is None else after)
 
 
 def mask_kernel(per_step, parts, me_ref, slab_ref, irrep_ref, occ_ref, virt_ref, row_ref, ints_ref, *refs):
@@ -227,11 +236,11 @@
     )(*parts, after)
 
 
-def contract_kernel(arrays, packed_other, last, start_ref, me_ref, home_ref, home_other_ref, ints_ref, *refs):
+def contract_kernel(arrays, packed_other, last, shared, which, slab_ref, me_ref, home_ref, home_other_ref, ints_ref, *refs):
     lhs = refs[-2] if last else refs[-1]
     count, rows, size = lhs.shape
     chips = count // 2 - 1
-    start = pl.multiple_of(start_ref[0], 128)
+    start = start_of(which, slab_ref, shared)
     home_first = home_other_ref.shape[1] - home_ref.shape[2]
     columns = pl.ds(start, size)
     lhs[0] = home_ref[0, :, columns]
@@ -258,13 +267,14 @@
     before_ref, out_ref, _, partial = refs
     me = me_ref[0]
     partial[...] = (total + before_ref[...]).reshape(partial.shape)
-    for p in range(count):
-        out_ref[p, :count] = partial[p ^ me]
-        for i in range(count):
-            out_ref[p, count + i : count + i + 1] = partial[i ^ me, p : p + 1]
-
-
-def contract(mine, others, home, home_other, ints, start, me, before=None, last=False, flops=0):
+    for i in range(count):
+        block = partial[i ^ me]
+        out_ref[i, :count] = block
+        for j in range(count):
+            out_ref[j, count + i : count + i + 1] = block[j : j + 1]
+
+
+def contract(mine, others, home, home_other, ints, me, slab, shared, which, before=None, last=False):
     occupied, size = mine[0].shape[-2:]
     cols = ints.shape[1]
     vmem = pl.BlockSpec(memory_space=pltpu.VMEM)
@@ -276,19 +286,19 @@
     else:
         out_shape = jax.ShapeDtypeStruct((occupied * occupied, cols), jnp.float32)
     return pl.pallas_call(
-        functools.partial(contract_kernel, len(mine), not others, last),
+        functools.partial(contract_kernel, len(mine), not others, last, shared, which),
         out_shape=out_shape,
         in_specs=[pl.BlockSpec(memory_space=pltpu.SMEM)] * 2 + [vmem] * (3 + len(operands)),
         out_specs=vmem,
         scratch_shapes=scratch,
         compiler_params=pltpu.CompilerParams(vmem_limit_bytes=4 * MIB + 16 * occupied * occupied * cols + 4 * occupied * occupied * size),
         cost_estimate=pl.CostEstimate(
-            flops=2 * occupied * occupied * size * cols + flops,
+            flops=2 * occupied * occupied * size * cols,
             bytes_accessed=2 * size * (cols + occupied * occupied),
             transcendentals=0,
         ),
         name="contract",
-    )(start, me, home, home_other, pltpu.with_memory_space_constraint(ints, pltpu.VMEM), *operands)
+    )(slab, me, home, home_other, pltpu.with_memory_space_constraint(ints, pltpu.VMEM), *operands)
 
 
 def select_exactly(values, select):
@@ -359,24 +369,18 @@
     slab_virt = slab_energy.shape[0]
     first_local = slab_virt // slab_count
     assert occ_local == 1
-    slab_index = lax.axis_index("slab").astype(jnp.int32)
     me = lax.axis_index("pair").astype(jnp.int32).reshape(1)
-    slab = slab_index.reshape(1)
+    slab = lax.axis_index("slab").astype(jnp.int32).reshape(1)
 
     shared = int(SHARE * rows_local) // 128 * 128
-    parity = slab_index % 2
-    own = (parity * shared).reshape(1)
-    other = ((1 - parity) * shared).reshape(1)
-    rest = jnp.full((1,), 2 * shared, jnp.int32)
-    whole = jnp.zeros((1,), jnp.int32)
     amps = amplitudes.reshape(occupied, virt_pairs)
     chips = [2 * k for k in range(1, pair_count // 2)]
 
-    parts = pack(amps, me, own, shared, pair_count, False)
+    parts = pack(amps, me, slab, shared, "own", pair_count)
     own_mine = [swap(part, "pair", bits) for part, bits in zip(parts, chips)]
-    parts = pack(amps, me, rest, rows_local - 2 * shared, pair_count, False, parts[-1])
+    parts = pack(amps, me, slab, shared, "rest", pair_count, parts[-1])
     rest_mine = [swap(part, "pair", bits) for part, bits in zip(parts, chips)]
-    (home,) = pack(amps, me, whole, rows_local, pair_count, True, parts[-1])
+    (home,) = pack(amps, me, slab, shared, "all", pair_count, parts[-1])
 
     own_mine, for_other = merge(own_mine, home)
     other_mine = swap(own_mine, "slab", 1)
@@ -384,9 +388,9 @@
     other_others = swap(other_mine, "pair", 1)
     masked, select, denominator = mask(integrals, me, slab, virt_irrep, occ_energy, slab_energy)
     rest_others = swap(for_other_core(rest_mine, denominator), "pair", 1)
-    partial = contract([own_mine], [], home, home_other, masked, own, me)
-    partial = contract(rest_mine, [rest_others], home, home_other, masked, rest, me, partial)
-    parts = contract([other_mine], [other_others], home, home_other, masked, other, me, partial, True)
+    partial = contract([own_mine], [], home, home_other, masked, me, slab, shared, "own")
+    partial = contract(rest_mine, [rest_others], home, home_other, masked, me, slab, shared, "rest", partial)
+    parts = contract([other_mine], [other_others], home, home_other, masked, me, slab, shared, "other", partial, True)
 
     parts = lax.all_to_all(parts, "pair", split_axis=0, concat_axis=0, tiled=True)
     ladder, mirror = add_parts(parts)

time: 61.2 us -> 51.2 us (0.84)
  local copies, waits for them, and re-layouts: 12.2 us -> 0 us
  waiting for transfers between devices: 8.08 us -> 12.6 us
  Pallas kernels: 17.3 us -> 14.3 us
  blocking collectives: 8.22 us -> 8.93 us
    unnamed x10 -> x0, local copies, waits for them, and re-layouts: 12.2 us -> none
    ppermute x13, waiting for transfers between devices: 8.08 us -> 12.6 us  [swap(): lax.ppermute(values, axis, [(p, p ^ bits) for p in range(lax.axis_size(ax...]
    pallas_call x3, Pallas kernels: 4.25 us -> 2.05 us  [contract(): pl.pallas_call(functools.partial(contract_kernel, len(mine), not others,...]
    pallas_call x1, Pallas kernels: 0.89 us -> 0.07 us  [merge(): pl.pallas_call(merge_kernel, out_shape=[jax.ShapeDtypeStruct((count,) + p...]
    all_to_all x1, blocking collectives: 8.22 us -> 8.93 us  [local(): lax.all_to_all(parts, 'pair', split_axis=0, concat_axis=0, tiled=True)]
  transfers between devices with their start and end apart: 13 -> 13, of which waited for: 4 -> 5; matrix products, arithmetic and copies ran while one was open for 0% -> 0% of each run, Pallas kernels for 21% -> 22%
where the time goes in v1:
time: 51.2 us; the launch traced here: 50.9 us
  starting transfers between devices  14.9 us (29%)
  Pallas kernels  14.3 us (28%)
  waiting for transfers between devices  12.6 us (25%)
  blocking collectives  8.93 us (17%)
    ppermute x13, starting transfers between devices, swap(): lax.ppermute(values, axis, [(p, p ^ bits) for p in range(lax.axis_size(ax...  14.9 us
    ppermute x13, waiting for transfers between devices, swap(): lax.ppermute(values, axis, [(p, p ^ bits) for p in range(lax.axis_size(ax...  12.6 us
    all_to_all x1, blocking collectives, local(): lax.all_to_all(parts, 'pair', split_axis=0, concat_axis=0, tiled=True)  8.93 us
    pallas_call x1, Pallas kernels, mask(): pl.pallas_call(functools.partial(mask_kernel, per_step, parts), grid=(chu...  6.35 us
    pallas_call x3, Pallas kernels, pack(): pl.pallas_call(functools.partial(pack_kernel, rows_local, shared, which),...  4.75 us
    pallas_call x3, Pallas kernels, contract(): pl.pallas_call(functools.partial(contract_kernel, len(mine), not others,...  2.05 us
    pallas_call x1, Pallas kernels, finish(): pl.pallas_call(finish_kernel, out_shape=jax.ShapeDtypeStruct((rows, first...  1.06 us
  transfers between devices with their start and end apart: 13, of which 5 were waited for; matrix products, arithmetic and copies ran while one was open for 0% of the time, Pallas kernels for 22%

profile of v1, /device:TPU:0, one launch (start us, length us, event | category | flops | bytes accessed | tf_op | source)
XLA Modules:
  0.0 50.9 jit_solution(5931249684619348348)
XLA Ops:
  0.0 1.6 %pack_amplitudes.2 = (bf16[2,8,4736]{2,1,0:T(8,128)(2,1)S(1)}, bf16[2,8,4736]{2,1,0:T(8,128)(2,1)S(1)}, bf16[2,8,4736]{2,1,0:T(8,128)(2,1)S(1)}) custom-call(s32[1]{0:T(128)} %bitcast.1.me_ref.after_ref, s32[1]{0:T(128)} %bitcast.slab_ref, bf16[8,160000]{1,0:T(8,128)(2,1)} %bitcast.10, s32[1]{0:T(128)} %bitcast.1.me_ref.after_ref), custom_call_target="tpu_custom_call" | custom-call | bytes 1212416 | tf_op jit(solution)/shard_map/pack_amplitudes/pallas_call | solution.py:67
  1.6 4.0 %collective-permute-start.2 = (bf16[2,8,4736]{2,1,0:T(8,128)(2,1)S(1)}, bf16[2,8,4736]{2,1,0:T(8,128)(2,1)S(1)}, u32[]{:S(2)}, u32[]{:S(2)}) collective-permute-start(bf16[2,8,4736]{2,1,0:T(8,128)(2,1)S(1)} %get-tuple-element.18.after_ref), channel_id=1, source_target_pairs={{0,24},{4,28},{8,16},{12,20},{16,8},{20,12},{24,0},{28,4},{1,25},{... | collective-permute-start | bytes 454664 | tf_op jit(solution)/shard_map/ppermute | solution.py:361
  5.5 0.5 %collective-permute-start = (bf16[2,8,4736]{2,1,0:T(8,128)(2,1)S(1)}, bf16[2,8,4736]{2,1,0:T(8,128)(2,1)S(1)}, u32[]{:S(2)}, u32[]{:S(2)}) collective-permute-start(bf16[2,8,4736]{2,1,0:T(8,128)(2,1)S(1)} %get-tuple-element.20), channel_id=1, source_target_pairs={{0,8},{4,12},{8,0},{12,4},{16,24},{20,28},{24,16},{28,20},{1,9},{5... | collective-permute-start | bytes 454664 | tf_op jit(solution)/shard_map/ppermute | solution.py:361
  6.2 1.8 %pack_amplitudes.3 = (bf16[2,8,10528]{2,1,0:T(8,128)(2,1)S(1)}, bf16[2,8,10528]{2,1,0:T(8,128)(2,1)S(1)}, bf16[2,8,10528]{2,1,0:T(8,128)(2,1)S(1)}) custom-call(s32[1]{0:T(128)} %bitcast.1.me_ref.after_ref, s32[1]{0:T(128)} %bitcast.slab_ref, bf16[8,160000]{1,0:T(8,128)(2,1)} %bitcast.11, bf16[2,8,4736]{2,1,0:T(8,128)(2,1)S(1)} %get-tuple-element.18.after_ref), custom_call_target="tpu_custom_call" | custom-call | bytes 2695168 | tf_op jit(solution)/shard_map/pack_amplitudes/pallas_call | solution.py:67
  8.0 2.9 %collective-permute-start.8 = (bf16[2,8,10528]{2,1,0:T(8,128)(2,1)S(1)}, bf16[2,8,10528]{2,1,0:T(8,128)(2,1)S(1)}, u32[]{:S(2)}, u32[]{:S(2)}) collective-permute-start(bf16[2,8,10528]{2,1,0:T(8,128)(2,1)S(1)} %get-tuple-element.19.after_ref), channel_id=1, source_target_pairs={{0,24},{4,28},{8,16},{12,20},{16,8},{20,12},{24,0},{28,4},{1,25},{... | collective-permute-start | bytes 1010696 | tf_op jit(solution)/shard_map/ppermute | solution.py:361
  10.9 0.5 %collective-permute-start.6 = (bf16[2,8,10528]{2,1,0:T(8,128)(2,1)S(1)}, bf16[2,8,10528]{2,1,0:T(8,128)(2,1)S(1)}, u32[]{:S(2)}, u32[]{:S(2)}) collective-permute-start(bf16[2,8,10528]{2,1,0:T(8,128)(2,1)S(1)} %get-tuple-element.25), channel_id=1, source_target_pairs={{0,8},{4,12},{8,0},{12,4},{16,24},{20,28},{24,16},{28,20},{1,9},{5... | collective-permute-start | bytes 1010696 | tf_op jit(solution)/shard_map/ppermute | solution.py:361
  11.5 1.3 %pack_home.1.refs_3_.home_ref = bf16[2,8,20000]{2,1,0:T(8,128)(2,1)S(1)} custom-call(s32[1]{0:T(128)} %bitcast.1.me_ref.after_ref, s32[1]{0:T(128)} %bitcast.slab_ref, bf16[8,160000]{1,0:T(8,128)(2,1)} %bitcast.12, bf16[2,8,10528]{2,1,0:T(8,128)(2,1)S(1)} %get-tuple-element.19.after_ref), custom_call_target="tpu_custom_call" | custom-call | bytes 1280000 | tf_op jit(solution)/shard_map/pack_home/pallas_call | solution.py:67
  12.8 0.2 collective-permute-start.7
  13.0 1.2 %collective-permute-done.refs_0_ = bf16[2,8,4736]{2,1,0:T(8,128)(2,1)S(1)} collective-permute-done((bf16[2,8,4736]{2,1,0:T(8,128)(2,1)S(1)}, bf16[2,8,4736]{2,1,0:T(8,128)(2,1)S(1)}, u32[]{:S(2)}, u32[]{:S(2)}) %collective-permute-start) | collective-permute-done | bytes 151584 | tf_op jit(solution)/shard_map/ppermute | solution.py:361
  14.3 1.6 %collective-permute-start.4 = (bf16[3,2,8,4736]{3,2,1,0:T(8,128)(2,1)S(1)}, bf16[3,2,8,4736]{3,2,1,0:T(8,128)(2,1)S(1)}, u32[]{:S(2)}, u32[]{:S(2)}) collective-permute-start(bf16[3,2,8,4736]{3,2,1,0:T(8,128)(2,1)S(1)} %get-tuple-element.24.refs_0_), channel_id=1, source_target_pairs={{0,1},{1,0},{2,3},{3,2},{4,5},{5,4},{6,7},{7,6},{8,9},{9,8},{10,11... | collective-permute-start | bytes 1363976 | tf_op jit(solution)/shard_map/ppermute | solution.py:361
  15.9 6.4 %mask_integrals.1 = (bf16[50,400,256]{2,1,0:T(8,128)(2,1)S(1)}, bf16[1024,256]{1,0:T(8,128)(2,1)S(1)}, f32[8,256]{1,0:T(8,128)S(1)}) custom-call(s32[1]{0:T(128)} %bitcast.1.me_ref.after_ref, s32[1]{0:T(128)} %bitcast.slab_ref, s32[400]{0:T(512)} %irrep_ref.1, f32[8]{0:T(128)} %occ_ref.1, f32[32]{0:T(128)} %virt_ref.1, s32[1,400]{1,0:T(1,128)} %bitcast.14, ...), custom_call_target="tpu_custom_call" | custom-call | flops 10000000000 | bytes 20480000 | tf_op jit(solution)/shard_map/mask_integrals/pallas_call | solution.py:157
  22.3 5.3 %collective-permute-done.6.refs_0_ = bf16[2,8,10528]{2,1,0:T(8,128)(2,1)S(1)} collective-permute-done((bf16[2,8,10528]{2,1,0:T(8,128)(2,1)S(1)}, bf16[2,8,10528]{2,1,0:T(8,128)(2,1)S(1)}, u32[]{:S(2)}, u32[]{:S(2)}) %collective-permute-start.6) | collective-permute-done | bytes 336928 | tf_op jit(solution)/shard_map/ppermute | solution.py:361
  27.8 0.5 collective-permute-start.5
  28.2 0.5 contract.3.refs_4_
  28.7 0.9 %collective-permute-done.9.refs_3_ = bf16[3,8,10528]{2,1,0:T(8,128)(2,1)S(1)} collective-permute-done((bf16[3,8,10528]{2,1,0:T(8,128)(2,1)S(1)}, bf16[3,8,10528]{2,1,0:T(8,128)(2,1)S(1)}, u32[]{:S(2)}, u32[]{:S(2)}) %collective-permute-start.9) | collective-permute-done | bytes 505376 | tf_op jit(solution)/shard_map/ppermute | solution.py:361
  29.6 1.1 %contract.4.refs_2_ = f32[64,256]{1,0:T(8,128)S(1)} custom-call(s32[1]{0:T(128)} %bitcast.slab_ref, s32[1]{0:T(128)} %bitcast.1.me_ref.after_ref, bf16[2,8,20000]{2,1,0:T(8,128)(2,1)S(1)} %pack_home.1.refs_3_.home_ref, bf16[8,34208]{1,0:T(8,128)(2,1)S(1)} %collective-permute-done.3.home_other_ref, bf16[20000,256]{1,0:T(8,128)(2,1)S(1)} %bitcast.8, ...), custom_call_target="tpu_custom_call" | custom-call | flops 344981504 | bytes 6737920 | tf_op jit(solution)/shard_map/contract/pallas_call | solution.py:288
  30.7 0.5 contract.5
  31.2 8.9 %all_to_all.5.parts_ref = f32[8,16,256]{2,1,0:T(8,128)S(1)} all-to-all(f32[8,16,256]{2,1,0:T(8,128)S(1)} %contract.5), channel_id=1, replica_groups=mesh['pair'=8,'slab'=4] {'pair'}, dimensions={0} | all-to-all | bytes 262144 | tf_op jit(solution)/shard_map/all_to_all | solution.py:395
  40.2 1.6 %collective-permute-start.10 = (f32[8,256]{1,0:T(8,128)S(1)}, f32[8,256]{1,0:T(8,128)S(1)}, u32[]{:S(2)}, u32[]{:S(2)}) collective-permute-start(f32[8,256]{1,0:T(8,128)S(1)} %get-tuple-element.30.refs_0_), channel_id=1, source_target_pairs={{0,1},{1,0},{2,3},{3,2},{4,5},{5,4},{6,7},{7,6},{8,9},{9,8},{10,11... | collective-permute-start | bytes 24584 | tf_op jit(solution)/shard_map/ppermute | solution.py:361
  41.8 2.6 %collective-permute-start.11 = (f32[8,256]{1,0:T(8,128)S(1)}, f32[8,256]{1,0:T(8,128)S(1)}, u32[]{:S(2)}, u32[]{:S(2)}) collective-permute-start(f32[8,256]{1,0:T(8,128)S(1)} %get-tuple-element.30.refs_0_), channel_id=1, source_target_pairs={{0,2},{1,3},{2,0},{3,1},{4,6},{5,7},{6,4},{7,5},{8,10},{9,11},{10,... | collective-permute-start | bytes 24584 | tf_op jit(solution)/shard_map/ppermute | solution.py:361
  44.4 0.2 collective-permute-start.12
  44.6 1.7 %collective-permute-done.11.refs_2_ = f32[8,256]{1,0:T(8,128)S(1)} collective-permute-done((f32[8,256]{1,0:T(8,128)S(1)}, f32[8,256]{1,0:T(8,128)S(1)}, u32[]{:S(2)}, u32[]{:S(2)}) %collective-permute-start.11) | collective-permute-done | bytes 8224 | tf_op jit(solution)/shard_map/ppermute | solution.py:361
  46.4 3.5 %collective-permute-done.12.refs_3_ = f32[8,256]{1,0:T(8,128)S(1)} collective-permute-done((f32[8,256]{1,0:T(8,128)S(1)}, f32[8,256]{1,0:T(8,128)S(1)}, u32[]{:S(2)}, u32[]{:S(2)}) %collective-permute-start.12) | collective-permute-done | bytes 8224 | tf_op jit(solution)/shard_map/ppermute | solution.py:361
  49.8 1.1 %finish.1 = f32[8,8,32]{2,1,0:T(8,128)} custom-call(f32[8,256]{1,0:T(8,128)S(1)} %get-tuple-element.28.ladder_ref, f32[8,256]{1,0:T(8,128)S(1)} %get-tuple-element.27.refs_3_.denominator_ref, bf16[1024,256]{1,0:T(8,128)(2,1)S(1)} %get-tuple-element.29.select_ref, f32[8,256]{1,0:T(8,128)S(1)} %get-tuple-element.30.refs_0_, ...), custom_call_target="tpu_custom_call" | custom-call | flops 12582912 | bytes 524288 | tf_op jit(solution)/shard_map/finish/pallas_call | solution.py:349
  (14 shorter events, 0.4 us)
Async XLA Ops:
  1.6 11.2 %collective-permute-start.2 = (bf16[2,8,4736]{2,1,0:T(8,128)(2,1)S(1)}, bf16[2,8,4736]{2,1,0:T(8,128)(2,1)S(1)}, u32[]{:S(2)}, u32[]{:S(2)}) collective-permute-start(bf16[2,8,4736]{2,1,0:T(8,128)(2,1)S(1)} %get-tuple-element.18.after_ref), channel_id=1, source_target_pairs={{0,24},{4,28},{8,16},{12,20},{16,8},{20,12},{24,0},{28,4},{1,25},{... | collective-permute-start | bytes 454664 | tf_op jit(solution)/shard_map/ppermute | solution.py:361
  5.5 8.6 %collective-permute-start = (bf16[2,8,4736]{2,1,0:T(8,128)(2,1)S(1)}, bf16[2,8,4736]{2,1,0:T(8,128)(2,1)S(1)}, u32[]{:S(2)}, u32[]{:S(2)}) collective-permute-start(bf16[2,8,4736]{2,1,0:T(8,128)(2,1)S(1)} %get-tuple-element.20), channel_id=1, source_target_pairs={{0,8},{4,12},{8,0},{12,4},{16,24},{20,28},{24,16},{28,20},{1,9},{5... | collective-permute-start | bytes 454664 | tf_op jit(solution)/shard_map/ppermute | solution.py:361
  6.1 8.1 %collective-permute-start.1 = (bf16[2,8,4736]{2,1,0:T(8,128)(2,1)S(1)}, bf16[2,8,4736]{2,1,0:T(8,128)(2,1)S(1)}, u32[]{:S(2)}, u32[]{:S(2)}) collective-permute-start(bf16[2,8,4736]{2,1,0:T(8,128)(2,1)S(1)} %get-tuple-element.21), channel_id=1, source_target_pairs={{0,16},{4,20},{8,24},{12,28},{16,0},{20,4},{24,8},{28,12},{1,17},{... | collective-permute-start | bytes 454664 | tf_op jit(solution)/shard_map/ppermute | solution.py:361
  8.0 14.3 %collective-permute-start.8 = (bf16[2,8,10528]{2,1,0:T(8,128)(2,1)S(1)}, bf16[2,8,10528]{2,1,0:T(8,128)(2,1)S(1)}, u32[]{:S(2)}, u32[]{:S(2)}) collective-permute-start(bf16[2,8,10528]{2,1,0:T(8,128)(2,1)S(1)} %get-tuple-element.19.after_ref), channel_id=1, source_target_pairs={{0,24},{4,28},{8,16},{12,20},{16,8},{20,12},{24,0},{28,4},{1,25},{... | collective-permute-start | bytes 1010696 | tf_op jit(solution)/shard_map/ppermute | solution.py:361
  10.9 16.7 %collective-permute-start.6 = (bf16[2,8,10528]{2,1,0:T(8,128)(2,1)S(1)}, bf16[2,8,10528]{2,1,0:T(8,128)(2,1)S(1)}, u32[]{:S(2)}, u32[]{:S(2)}) collective-permute-start(bf16[2,8,10528]{2,1,0:T(8,128)(2,1)S(1)} %get-tuple-element.25), channel_id=1, source_target_pairs={{0,8},{4,12},{8,0},{12,4},{16,24},{20,28},{24,16},{28,20},{1,9},{5... | collective-permute-start | bytes 1010696 | tf_op jit(solution)/shard_map/ppermute | solution.py:361
  12.8 14.8 %collective-permute-start.7 = (bf16[2,8,10528]{2,1,0:T(8,128)(2,1)S(1)}, bf16[2,8,10528]{2,1,0:T(8,128)(2,1)S(1)}, u32[]{:S(2)}, u32[]{:S(2)}) collective-permute-start(bf16[2,8,10528]{2,1,0:T(8,128)(2,1)S(1)} %get-tuple-element.26), channel_id=1, source_target_pairs={{0,16},{4,20},{8,24},{12,28},{16,0},{20,4},{24,8},{28,12},{1,17},{... | collective-permute-start | bytes 1010696 | tf_op jit(solution)/shard_map/ppermute | solution.py:361
  14.2 14.0 %collective-permute-start.3 = (bf16[8,34208]{1,0:T(8,128)(2,1)S(1)}, bf16[8,34208]{1,0:T(8,128)(2,1)S(1)}, u32[]{:S(2)}, u32[]{:S(2)}) collective-permute-start(bf16[8,34208]{1,0:T(8,128)(2,1)S(1)} %get-tuple-element.22), channel_id=1, source_target_pairs={{0,4},{4,0},{8,12},{12,8},{16,20},{20,16},{24,28},{28,24},{1,5},{5... | collective-permute-start | bytes 1641992 | tf_op jit(solution)/shard_map/ppermute | solution.py:361
  14.3 13.4 %collective-permute-start.4 = (bf16[3,2,8,4736]{3,2,1,0:T(8,128)(2,1)S(1)}, bf16[3,2,8,4736]{3,2,1,0:T(8,128)(2,1)S(1)}, u32[]{:S(2)}, u32[]{:S(2)}) collective-permute-start(bf16[3,2,8,4736]{3,2,1,0:T(8,128)(2,1)S(1)} %get-tuple-element.24.refs_0_), channel_id=1, source_target_pairs={{0,1},{1,0},{2,3},{3,2},{4,5},{5,4},{6,7},{7,6},{8,9},{9,8},{10,11... | collective-permute-start | bytes 1363976 | tf_op jit(solution)/shard_map/ppermute | solution.py:361
  27.7 2.0 %collective-permute-start.9 = (bf16[3,8,10528]{2,1,0:T(8,128)(2,1)S(1)}, bf16[3,8,10528]{2,1,0:T(8,128)(2,1)S(1)}, u32[]{:S(2)}, u32[]{:S(2)}) collective-permute-start(bf16[3,8,10528]{2,1,0:T(8,128)(2,1)S(1)} %for_other_core.1), channel_id=1, source_target_pairs={{0,4},{4,0},{8,12},{12,8},{16,20},{20,16},{24,28},{28,24},{1,5},{5... | collective-permute-start | bytes 1516040 | tf_op jit(solution)/shard_map/ppermute | solution.py:361
  27.8 3.0 %collective-permute-start.5 = (bf16[3,2,8,4736]{3,2,1,0:T(8,128)(2,1)S(1)}, bf16[3,2,8,4736]{3,2,1,0:T(8,128)(2,1)S(1)}, u32[]{:S(2)}, u32[]{:S(2)}) collective-permute-start(bf16[3,2,8,4736]{3,2,1,0:T(8,128)(2,1)S(1)} %collective-permute-done.4.refs_0_), channel_id=1, source_target_pairs={{0,4},{4,0},{8,12},{12,8},{16,20},{20,16},{24,28},{28,24},{1,5},{5... | collective-permute-start | bytes 1363976 | tf_op jit(solution)/shard_map/ppermute | solution.py:361
  40.2 4.5 %collective-permute-start.10 = (f32[8,256]{1,0:T(8,128)S(1)}, f32[8,256]{1,0:T(8,128)S(1)}, u32[]{:S(2)}, u32[]{:S(2)}) collective-permute-start(f32[8,256]{1,0:T(8,128)S(1)} %get-tuple-element.30.refs_0_), channel_id=1, source_target_pairs={{0,1},{1,0},{2,3},{3,2},{4,5},{5,4},{6,7},{7,6},{8,9},{9,8},{10,11... | collective-permute-start | bytes 24584 | tf_op jit(solution)/shard_map/ppermute | solution.py:361
  41.8 4.5 %collective-permute-start.11 = (f32[8,256]{1,0:T(8,128)S(1)}, f32[8,256]{1,0:T(8,128)S(1)}, u32[]{:S(2)}, u32[]{:S(2)}) collective-permute-start(f32[8,256]{1,0:T(8,128)S(1)} %get-tuple-element.30.refs_0_), channel_id=1, source_target_pairs={{0,2},{1,3},{2,0},{3,1},{4,6},{5,7},{6,4},{7,5},{8,10},{9,11},{10,... | collective-permute-start | bytes 24584 | tf_op jit(solution)/shard_map/ppermute | solution.py:361
  44.4 5.4 %collective-permute-start.12 = (f32[8,256]{1,0:T(8,128)S(1)}, f32[8,256]{1,0:T(8,128)S(1)}, u32[]{:S(2)}, u32[]{:S(2)}) collective-permute-start(f32[8,256]{1,0:T(8,128)S(1)} %get-tuple-element.30.refs_0_), channel_id=1, source_target_pairs={{0,3},{1,2},{2,1},{3,0},{4,7},{5,6},{6,5},{7,4},{8,11},{9,10},{10,... | collective-permute-start | bytes 24584 | tf_op jit(solution)/shard_map/ppermute | solution.py:361
